TPU v7x, 32 devices: a whole 2x2x4 slice. The times are simulated.
32 devices in a mesh: groups: 2 (over y), tensor: 4 (over z), expert: 4 (over x, core).
Axes of the slice: x: 2, y: 2, z: 4, core: 2. Of those that a mesh axis runs over, the one named last changes fastest.
Arguments:
- center: bfloat16 [32, 6144], P(('groups', 'expert')), parts along dimension 0, may hold values from -6 to 6
- gens: bfloat16 [32, 64, 6144], P(('groups', 'expert'), 'tensor'), parts along dimension 0, may hold values from -3 to 3
- query: bfloat16 [32, 6144], P(('groups', 'expert')), parts along dimension 0, may hold values from -6 to 6
- routes: int32 [32, 2], P(('groups', 'expert')), parts along dimension 0, may hold values from 0 to 3, as said below
- route_weights: float32 [32, 2], P(('groups', 'expert')), parts along dimension 0, may hold values from 0.25 to 1
- gate_weight: bfloat16 [4, 6144, 8192], P('expert', None, 'tensor'), may hold values from -0.078125 to 0.078125
- up_weight: bfloat16 [4, 6144, 8192], P('expert', None, 'tensor'), may hold values from -0.078125 to 0.078125
- down_weight: bfloat16 [4, 8192, 6144], P('expert', 'tensor'), may hold values from -0.0625 to 0.0625
- block_mask: int32 [4, 3, 48, 64], P('expert', None, None, 'tensor'), may hold values 0 or 1
Outputs:
- center_out: bfloat16 [32, 6144], P(('groups', 'expert')), parts along dimension 0
- gens_out: bfloat16 [32, 64, 6144], P(('groups', 'expert'), 'tensor'), parts along dimension 0
- radius: float32 [32, 6144], P(('groups', 'expert')), parts along dimension 0
- adjoint: float32 [32, 6144], P(('groups', 'expert')), parts along dimension 0
There are 2 independent parts, one for each index of `groups`. A program takes and returns all parts, laid end to end along the dimension named above; an argument that names none is the same for every part. Nothing has to cross between parts.
Inputs may be any that keep to these rules, and one draw needn't show every extreme that they name: `routes`: each token names two different experts. In every aligned block of 4 tokens (those of one index of expert), no expert is named by more than 3 tokens, and one expert, the same in all blocks of a draw, is named by exactly 3.
All inputs are finite; a program needn't handle non-finite values. No bound on the sum of `block_mask` on one device may be relied on, other than what follows from the above.
Results may differ from a plain program's by a relative error of at most 0.0075.
Values may be sent and summed in bfloat16 or wider, within the bound.
A program may use at most 512 MiB of HBM per device.

v0:
```python
import jax
import jax.numpy as jnp
from jax import lax
from jax.sharding import PartitionSpec as P

BLK = 128
MOST = 3


def shards(
    center, gens, query, routes, route_weights, gate_weight, up_weight, down_weight, block_mask
):
    experts = lax.axis_size("expert")
    slots = experts * MOST
    rows_here = gens.shape[1]
    width = gens.shape[2]
    hidden_here = gate_weight.shape[2]
    expert_ids = jnp.arange(experts, dtype=jnp.int32)
    named = (routes[:, :, None] == expert_ids[None, None, :]).astype(jnp.int32)
    per_token = jnp.sum(named, axis=1)
    earlier = jnp.cumsum(per_token, axis=0) - per_token
    slot_of = jnp.sum(named * earlier[:, None, :], axis=2)
    target = routes * MOST + slot_of
    slot_ids = jnp.arange(slots, dtype=jnp.int32)
    hits = (target[:, :, None] == slot_ids[None, None, :]).astype(jnp.float32)
    select = jnp.sum(hits, axis=1).astype(jnp.bfloat16)
    combine_weights = jnp.sum(hits * route_weights[:, :, None], axis=1)
    send_gens = jnp.einsum("bs,brd->srd", select, gens, preferred_element_type=jnp.float32).astype(
        jnp.bfloat16
    )
    pair_in = jnp.stack([center, query], axis=1)
    send_pair = jnp.einsum(
        "bs,brd->srd", select, pair_in, preferred_element_type=jnp.float32
    ).astype(jnp.bfloat16)
    recv_gens, recv_pair = (
        lax.all_to_all(
            send_gens.reshape(experts, MOST, rows_here, width),
            "expert",
            split_axis=0,
            concat_axis=0,
            tiled=True,
        ),
        lax.all_to_all(
            send_pair.reshape(experts, MOST, 2, width),
            "expert",
            split_axis=0,
            concat_axis=0,
            tiled=True,
        ),
    )
    recv_gens = recv_gens.reshape(slots, rows_here, width)
    recv_pair = recv_pair.reshape(slots, 2, width)
    mask_here = block_mask[0].astype(jnp.bfloat16)
    width_blocks = width // BLK
    hidden_blocks = hidden_here // BLK
    gate_masked = (
        gate_weight[0].reshape(width_blocks, BLK, hidden_blocks, BLK)
        * mask_here[0][:, None, :, None]
    ).reshape(width, hidden_here)
    up_masked = (
        up_weight[0].reshape(width_blocks, BLK, hidden_blocks, BLK) * mask_here[1][:, None, :, None]
    ).reshape(width, hidden_here)
    down_masked = (
        down_weight[0].reshape(hidden_blocks, BLK, width_blocks, BLK)
        * mask_here[2].T[:, None, :, None]
    ).reshape(hidden_here, width)
    both_in = jnp.concatenate([gate_masked, up_masked], axis=1)
    gen_pre = jnp.einsum(
        "srd,dh->srh",
        lax.all_gather(recv_gens, "tensor", axis=1, tiled=True),
        both_in,
        preferred_element_type=jnp.float32,
    )
    center_pre = jnp.dot(recv_pair[:, 0], both_in, preferred_element_type=jnp.float32)
    gate_center = center_pre[:, :hidden_here]
    up_center = center_pre[:, hidden_here:]
    sigma = 1.0 / (1.0 + jnp.exp(-gate_center))
    activated = gate_center * sigma
    slope_gate = sigma * (1.0 + gate_center * (1.0 - sigma)) * up_center
    hidden_center = (activated * up_center).astype(jnp.bfloat16)
    hidden_gens = (
        slope_gate[:, None, :] * gen_pre[:, :, :hidden_here]
        + activated[:, None, :] * gen_pre[:, :, hidden_here:]
    ).astype(jnp.bfloat16)
    out_center = jnp.dot(hidden_center, down_masked, preferred_element_type=jnp.float32)
    adjoint_hidden = jnp.einsum(
        "sd,hd->sh", recv_pair[:, 1], down_masked, preferred_element_type=jnp.float32
    )
    adjoint_pre = jnp.concatenate(
        [
            (adjoint_hidden * slope_gate).astype(jnp.bfloat16),
            (adjoint_hidden * activated).astype(jnp.bfloat16),
        ],
        axis=1,
    )
    adjoint_in = jnp.einsum("sh,dh->sd", adjoint_pre, both_in, preferred_element_type=jnp.float32)
    pair_out = jnp.stack([out_center, adjoint_in], axis=0)
    out_gens = jnp.einsum(
        "srh,hd->rsd", hidden_gens, down_masked, preferred_element_type=jnp.float32
    )
    all_rows = out_gens.shape[0]
    back_gens, back_pair = (
        lax.all_to_all(
            out_gens.reshape(all_rows, experts, MOST, width),
            "expert",
            split_axis=1,
            concat_axis=1,
            tiled=True,
        ),
        lax.all_to_all(
            pair_out.reshape(2, experts, MOST, width),
            "expert",
            split_axis=1,
            concat_axis=1,
            tiled=True,
        ),
    )
    gens_partial = jnp.einsum(
        "bs,rsd->brd",
        combine_weights,
        back_gens.reshape(all_rows, slots, width),
        precision=lax.Precision.HIGHEST,
    )
    pair_partial = jnp.einsum(
        "bs,rsd->rbd",
        combine_weights,
        back_pair.reshape(2, slots, width),
        precision=lax.Precision.HIGHEST,
    )
    token_gens = lax.psum_scatter(gens_partial, "tensor", scatter_dimension=1, tiled=True)
    token_pair = lax.psum(pair_partial, "tensor")
    radius_part = jnp.sum(jnp.abs(token_gens), axis=1)
    radius = lax.psum(radius_part.astype(jnp.bfloat16), "tensor").astype(jnp.float32)
    return (
        token_pair[0].astype(jnp.bfloat16),
        token_gens.astype(jnp.bfloat16),
        radius,
        token_pair[1],
    )


def solution(mesh):
    placed = (
        P(("groups", "expert"), None),
        P(("groups", "expert"), "tensor", None),
        P(("groups", "expert"), None),
        P(("groups", "expert"), None),
        P(("groups", "expert"), None),
        P("expert", None, "tensor"),
        P("expert", None, "tensor"),
        P("expert", "tensor", None),
        P("expert", None, None, "tensor"),
    )
    return jax.shard_map(
        shards,
        mesh=mesh,
        in_specs=placed,
        out_specs=(
            P(("groups", "expert"), None),
            P(("groups", "expert"), "tensor", None),
            P(("groups", "expert"), None),
            P(("groups", "expert"), None),
        ),
        check_vma=False,
    )
```

profile of v0, /device:TPU:0, one launch (start us, length us, event | category | flops | bytes accessed | tf_op | source)
XLA Modules:
  0.0 819.5 jit_solution(17590940010263337281)
XLA Ops:
  7.2 0.8 convert_reduce_fusion.1
  8.1 0.9 select_reduce_fusion.1
  8.9 0.7 multiply_add_fusion
  9.6 1.3 select_reduce_fusion
  11.0 1.4 convolution_convert_fusion
  12.4 2.7 copy.88
  15.1 4.2 all-to-all-start.2
  19.3 0.7 convert_element_type.48
  20.1 0.1 copy.81
  20.1 0.1 copy.82
  20.2 1.1 convolution_convert_fusion.1
  21.4 1.0 copy.80
  22.4 25.4 %all-to-all-done.2 = bf16[4,3,16,6144]{3,2,1,0:T(8,128)(2,1)S(1)} async-done(((bf16[4,3,16,6144]{3,2,1,0:T(8,128)(2,1)}), bf16[4,3,16,6144]{3,2,1,0:T(8,128)(2,1)S(1)}, u32[]{:S(2)}, u32[]{:S(2)}) %all-to-all-start.2) | async-done | bytes 2359328 | tf_op jit(solution)/shard_map/all_to_all | solution.py:36
  47.8 3.5 all-to-all-start
  51.3 0.2 all-gather.2.cloned.1.call-start
  51.5 0.5 all-gather.2.cloned.1.call-update
  52.0 4.3 mul.105
  56.3 9.4 %mul.109 = bf16[48,128,16,128]{3,2,1,0:T(8,128)(2,1)} broadcast(bf16[48,16]{1,0:T(8,128)(2,1)S(1)} %copy.82), dimensions={0,2} | broadcast | bytes 25167360 | tf_op jit(solution)/shard_map/mul | solution.py:61
  65.7 43.0 %bitcast_multiply_fusion.1 = (bf16[6144,2048]{1,0:T(8,128)(2,1)}, bf16[6144,2048]{1,0:T(8,128)(2,1)}) fusion(bf16[768,8,16,128]{3,2,1,0:T(8,128)(2,1)} %bitcast.94, bf16[1,6144,2048]{2,1,0:T(8,128)(2,1)} %param.15, bf16[768,8,16,128]{3,2,1,0:T(8,128)(2,1)S(1)} %bitcast.93, bf16[1,6144,2048]{2,1,0:T(8,128)(2,1)} %param.14), kind=kLoop, calls=%fused_computation.7 | loop fusion | flops 25165824 | bytes 150994944 | tf_op jit(solution)/shard_map/mul | solution.py:61
  108.7 8.9 %mul.114 = bf16[16,128,48,128]{3,2,1,0:T(8,128)(2,1)} broadcast(bf16[16,48]{1,0:T(8,128)(2,1)S(1)} %get-tuple-element.39), dimensions={0,2} | broadcast | bytes 25167360 | tf_op jit(solution)/shard_map/mul | solution.py:64
  117.6 35.5 %mul.115 = bf16[1,2048,6144]{2,1,0:T(8,128)(2,1)} reshape(bf16[16,128,48,128]{3,2,1,0:T(8,128)(2,1)} %mul.114) | data formatting | bytes 50331648 | tf_op jit(solution)/shard_map/mul | solution.py:64
  153.1 0.4 fusion.50
  153.5 17.6 %fusion.14 = f32[12,4096]{1,0:T(8,128)S(1)} fusion(bf16[6144,2048]{1,0:T(8,128)(2,1)} %get-tuple-element.42, bf16[6144,2048]{1,0:T(8,128)(2,1)} %get-tuple-element.43, bf16[12,1,6144]{2,1,0:T(2,128)(2,1)S(1)} %get-tuple-element.35), kind=kOutput, calls=%fused_computation.17 | convolution fusion | flops 704643072 | bytes 50675712 | tf_op jit(solution)/shard_map/dot_general | solution.py:74
  171.1 18.1 %multiply_convert_fusion.1 = (bf16[12,2048]{1,0:T(8,128)(2,1)S(1)}, f32[12,2048]{1,0:T(8,128)S(1)}, bf16[12,2048]{1,0:T(8,128)(2,1)S(1)}, f32[12,2048]{1,0:T(8,128)S(1)}, bf16[12,2048]{1,0:T(8,128)(2,1)S(1)}) fusion(f32[12,4096]{1,0:T(8,128)S(1)} %fusion.14, bf16[1,2048,6144]{2,1,0:T(8,128)(2,1)} %param.16, bf16[1,2048,6144]{2,1,0:T(8,128)(2,1)} %mul.115, ...), kind=kOutput, calls=%fused_computation.43 | convolution fusion | flops 314941440 | bytes 51019776 | tf_op jit(solution)/shard_map/sd,hd->sh/dot_general | solution.py:86
  189.2 19.9 %fusion.13 = f32[12,6144]{1,0:T(8,128)S(1)} fusion(bf16[6144,2048]{1,0:T(8,128)(2,1)} %get-tuple-element.42, bf16[6144,2048]{1,0:T(8,128)(2,1)} %get-tuple-element.43, bf16[12,2048]{1,0:T(8,128)(2,1)S(1)} %get-tuple-element.34, bf16[12,2048]{1,0:T(8,128)(2,1)S(1)} %get-tuple-element.32), kind=kOutput, calls=%fused_computation.16 | convolution fusion | flops 704839680 | bytes 50724864 | tf_op jit(solution)/shard_map/sh,dh->sd/dot_general | solution.py:96
  209.2 0.1 stack.19
  209.3 0.2 copy.84
  209.5 16.8 %fusion.17 = f32[1,4,3,6144]{3,1,2,0:T(4,128)S(1)} fusion(bf16[1,2048,6144]{2,1,0:T(8,128)(2,1)} %param.16, bf16[1,2048,6144]{2,1,0:T(8,128)(2,1)} %mul.115, bf16[4,3,2048]{2,1,0:T(4,128)(2,1)S(1)} %reshape.80), kind=kOutput, calls=%fused_computation.22 | convolution fusion | flops 314572800 | bytes 50675712 | tf_op jit(solution)/shard_map/dot_general | solution.py:85
  226.3 0.1 pad_maximum_fusion.4
  226.5 1.3 copy.85
  227.7 3.7 all-to-all-start.1
  231.4 0.0 all-gather.2.cloned.1.call-done
  231.5 47.7 %fusion = f32[12,64,4096]{2,1,0:T(8,128)} fusion(bf16[12,64,6144]{2,1,0:T(8,128)(2,1)} %all-gather.2.cloned.1.call-done, bf16[6144,2048]{1,0:T(8,128)(2,1)} %get-tuple-element.42, bf16[6144,2048]{1,0:T(8,128)(2,1)} %get-tuple-element.43), kind=kOutput, calls=%fused_computation.1 | convolution fusion | flops 38755368960 | bytes 72351744 | tf_op jit(solution)/shard_map/srd,dh->srh/dot_general | solution.py:68
  279.1 32.4 %fusion.3 = f32[6144,12,64]{0,2,1:T(8,128)} fusion(bf16[256,8,48,128]{3,2,1,0:T(8,128)(2,1)} %bitcast.92, bf16[1,2048,6144]{2,1,0:T(8,128)(2,1)} %param.16, f32[12,64,4096]{2,1,0:T(8,128)} %fusion, f32[12,2048]{1,0:T(8,128)S(1)} %get-tuple-element.37, f32[12,2048]{1,0:T(8,128)S(1)} %get-tuple-element.33), kind=kOutput, calls=%fused_computation.5 | convolution fusion | flops 19383975936 | bytes 81985536 | tf_op jit(solution)/shard_map/srh,hd->rsd/dot_general | solution.py:98
  311.6 7.4 all-to-all-start.3
  319.0 0.3 all-reduce.4.cloned.1.call-start
  319.3 1.7 convolution_bitcast_fusion
  321.1 203.5 %all-to-all-done.3 = f32[64,4,3,6144]{3,0,2,1:T(8,128)} async-done(((f32[64,4,3,6144]{3,0,2,1:T(8,128)}), f32[64,4,3,6144]{3,0,2,1:T(8,128)}, u32[]{:S(2)}, u32[]{:S(2)}) %all-to-all-start.3) | async-done | bytes 18874400 | tf_op jit(solution)/shard_map/all_to_all | solution.py:103
  524.5 31.7 %fusion.11 = f32[4,64,6144]{2,0,1:T(4,128)} fusion(f32[64,12,6144]{2,0,1:T(8,128)} %bitcast.25, f32[4,12]{1,0:T(4,128)S(1)} %copy-done.3), kind=kOutput, calls=%fused_computation.14 | convolution fusion | flops 226492416 | bytes 25166016 | tf_op jit(solution)/shard_map/bs,rsd->brd/dot_general | solution.py:118
  556.3 0.6 dynamic-slice
  557.5 229.5 %all-reduce.4.cloned.1.call-done = (f32[2,4,6144]{2,1,0:T(4,128)}, f32[4,64,6144]{2,0,1:T(4,128)}) async-done(((f32[2,4,6144]{2,1,0:T(4,128)}, f32[4,64,6144]{2,0,1:T(4,128)}), (f32[2,4,6144]{2,1,0:T(4,128)}, f32[4,64,6144]{2,0,1:T(4,128)})) %all-reduce.4.cloned.1.call-update) | async-done | bytes 6488080 | tf_op jit(solution)/shard_map/psum | solution.py:131
  787.0 1.7 dynamic-slice_convert_fusion
  788.8 1.9 abs_reduce_fusion
  790.6 1.5 slice_bitcast_fusion
  792.2 1.5 fusion.38
  793.7 1.3 copy.90
  795.0 17.0 %psum.15 = bf16[4,6144]{1,0:T(4,128)(2,1)S(1)} all-reduce(bf16[4,6144]{1,0:T(4,128)(2,1)S(1)} %abs_reduce_fusion), channel_id=1, replica_groups=mesh['groups'=2,'tensor'=4,'expert'=4] {'tensor'}, use_global_device_ids=true, to_apply=%region_8.9 | all-reduce | flops 24576 | bytes 98304 | tf_op jit(solution)/shard_map/psum | solution.py:133
  812.1 0.7 convert_element_type.57
  (17 shorter events, 0.1 us)
Async XLA Ops:
  7.2 3.8 copy-start
  15.1 32.7 %all-to-all-start.2 = ((bf16[4,3,16,6144]{3,2,1,0:T(8,128)(2,1)}), bf16[4,3,16,6144]{3,2,1,0:T(8,128)(2,1)S(1)}, u32[]{:S(2)}, u32[]{:S(2)}) async-start(bf16[4,3,16,6144]{3,2,1,0:T(8,128)(2,1)} %bitcast.97), calls=%async_computation.2 | async-start | bytes 4718592 | tf_op jit(solution)/shard_map/all_to_all | solution.py:36
  47.8 3.7 copy-start.2
  47.8 105.3 %all-to-all-start = ((bf16[4,3,2,6144]{3,2,1,0:T(2,128)(2,1)}), bf16[4,3,2,6144]{3,2,1,0:T(2,128)(2,1)S(1)}, u32[]{:S(2)}, u32[]{:S(2)}) async-start(bf16[4,3,2,6144]{3,2,1,0:T(2,128)(2,1)} %bitcast.3), calls=%async_computation | async-start | bytes 589824 | tf_op jit(solution)/shard_map/all_to_all | solution.py:43
  51.3 180.2 %all-gather.2.cloned.1.call-start = ((), (), s32[]{:S(2)}) async-start(), calls=%async_computation.4 | async-start | bytes 11796480 | tf_op jit(solution)/shard_map/all_gather | solution.py:70
  227.7 83.9 %all-to-all-start.1 = ((f32[2,4,3,6144]{3,0,2,1:T(2,128)}), f32[2,4,3,6144]{3,0,2,1:T(2,128)S(1)}, u32[]{:S(2)}, u32[]{:S(2)}) async-start(f32[2,4,3,6144]{3,0,2,1:T(2,128)} %copy.85), calls=%async_computation.1 | async-start | bytes 1179648 | tf_op jit(solution)/shard_map/all_to_all | solution.py:110
  311.6 7.7 copy-start.3
  311.6 212.9 %all-to-all-start.3 = ((f32[64,4,3,6144]{3,0,2,1:T(8,128)}), f32[64,4,3,6144]{3,0,2,1:T(8,128)}, u32[]{:S(2)}, u32[]{:S(2)}) async-start(f32[64,4,3,6144]{3,0,2,1:T(8,128)} %bitcast.95), calls=%async_computation.3 | async-start | bytes 37748736 | tf_op jit(solution)/shard_map/all_to_all | solution.py:103
  319.0 237.3 %copy-start.4 = (u32[32]{0:T(128)S(1)}, u32[32]{0:T(128)}, u32[]{:S(2)}) copy-start(u32[32]{0:T(128)} %constant.24) | copy-start | bytes 388
  319.0 493.7 %copy-start.1 = (bf16[4,16,6144]{2,1,0:T(8,128)(2,1)S(1)}, bf16[4,16,6144]{2,1,0:T(8,128)(2,1)}, u32[]{:S(2)}) copy-start(bf16[4,16,6144]{2,1,0:T(8,128)(2,1)} %param.10) | copy-start | bytes 2359300
  319.0 468.0 %all-reduce.4.cloned.1.call-start = ((), (), s32[]{:S(2)}) async-start(), calls=%async_computation.5 | async-start | bytes 12976128 | tf_op jit(solution)/shard_map/psum | solution.py:131
Sparse Core Ops, SparseCore 0:
  53.7 169.3 all-gather.1
  556.4 230.6 all-reduce.3
where the time goes:
time: 821 us; the launch traced here: 820 us
  waiting for transfers between devices  459 us (56%)
  matrix products  188 us (23%)
  local copies, waits for them, and re-layouts  70.8 us (9%)
  other arithmetic  50.2 us (6%)
  starting transfers between devices  19.3 us (2%)
  blocking collectives  17 us (2%)
  between operations  14.9 us (2%)
    psum x1, waiting for transfers between devices, shards(): token_pair = lax.psum(pair_partial, 'tensor')  230 us
    all_to_all x1, waiting for transfers between devices, shards(): lax.all_to_all(out_gens.reshape(all_rows, experts, MOST, width), 'expert'...  203 us
    dot_general x1, matrix products, shards(): jnp.einsum('srd,dh->srh', lax.all_gather(recv_gens, 'tensor', axis=1, til...  47.7 us
    mul x2, local copies, waits for them, and re-layouts, shards(): down_weight[0].reshape(hidden_blocks, BLK, width_blocks, BLK)  44.4 us
    mul x1, other arithmetic, shards(): up_weight[0].reshape(width_blocks, BLK, hidden_blocks, BLK)  43 us
    dot_general x1, matrix products, shards(): jnp.einsum('srh,hd->rsd', hidden_gens, down_masked, preferred_element_typ...  32.4 us
    dot_general x1, matrix products, shards(): jnp.einsum('bs,rsd->brd', combine_weights, back_gens.reshape(all_rows, sl...  31.7 us
    all_to_all x1, waiting for transfers between devices, shards(): lax.all_to_all(send_gens.reshape(experts, MOST, rows_here, width), 'exper...  25.4 us
  transfers between devices with their start and end apart: 6, of which 3 were waited for; matrix products, arithmetic and copies ran while one was open for 32% of the time, Pallas kernels for 0%

commit v1 on v0

--- a/solution.py
+++ b/solution.py
@@ -100,12 +100,20 @@
     )
     all_rows = out_gens.shape[0]
     back_gens, back_pair = (
-        lax.all_to_all(
-            out_gens.reshape(all_rows, experts, MOST, width),
-            "expert",
-            split_axis=1,
-            concat_axis=1,
-            tiled=True,
+        jnp.concatenate(
+            lax.all_to_all(
+                jnp.stack(
+                    jnp.split(
+                        out_gens.reshape(all_rows, experts, MOST, width),
+                        lax.axis_size("expert"),
+                        axis=1,
+                    )
+                ),
+                "expert",
+                0,
+                0,
+            ),
+            axis=1,
         ),
         lax.all_to_all(
             pair_out.reshape(2, experts, MOST, width),

time: 821 us -> 840 us (1.023)
  local copies, waits for them, and re-layouts: 70.8 us -> 80.4 us
    another operation x1 -> x2, local copies, waits for them, and re-layouts: 0.04 us -> 9.54 us  [the longest x1 9.5 us: shards(): jnp.stack(jnp.split(out_gens.reshape(all_rows, experts, MOST, width), lax...]
    another operation x0 -> x1, other arithmetic: none -> 8.47 us  [shards(): jnp.stack(jnp.split(out_gens.reshape(all_rows, experts, MOST, width), lax...]
  transfers between devices with their start and end apart: 6 -> 6, of which waited for: 3 -> 3; matrix products, arithmetic and copies ran while one was open for 32% -> 33% of each run, Pallas kernels for 0% -> 0%
where the time goes in v1:
time: 840 us; the launch traced here: 838 us
  waiting for transfers between devices  458 us (55%)
  matrix products  189 us (22%)
  local copies, waits for them, and re-layouts  80.4 us (10%)
  other arithmetic  58.6 us (7%)
  starting transfers between devices  20 us (2%)
  blocking collectives  17 us (2%)
  between operations  14.9 us (2%)
    psum x1, waiting for transfers between devices, shards(): token_pair = lax.psum(pair_partial, 'tensor')  230 us
    all_to_all x1, waiting for transfers between devices, shards(): lax.all_to_all(jnp.stack(jnp.split(out_gens.reshape(all_rows, experts, MO...  202 us
    dot_general x1, matrix products, shards(): jnp.einsum('srd,dh->srh', lax.all_gather(recv_gens, 'tensor', axis=1, til...  47.7 us
    mul x2, local copies, waits for them, and re-layouts, shards(): down_weight[0].reshape(hidden_blocks, BLK, width_blocks, BLK)  44.5 us
    mul x1, other arithmetic, shards(): up_weight[0].reshape(width_blocks, BLK, hidden_blocks, BLK)  43 us
    dot_general x1, matrix products, shards(): jnp.einsum('srh,hd->rsd', hidden_gens, down_masked, preferred_element_typ...  32.4 us
    dot_general x1, matrix products, shards(): jnp.einsum('bs,rsd->brd', combine_weights, back_gens.reshape(all_rows, sl...  31.6 us
    all_to_all x1, waiting for transfers between devices, shards(): lax.all_to_all(send_gens.reshape(experts, MOST, rows_here, width), 'exper...  25.4 us
  transfers between devices with their start and end apart: 6, of which 3 were waited for; matrix products, arithmetic and copies ran while one was open for 33% of the time, Pallas kernels for 0%

profile of v1, /device:TPU:0, one launch (start us, length us, event | category | flops | bytes accessed | tf_op | source)
XLA Modules:
  0.0 838.3 jit_solution(708217226540127472)
XLA Ops:
  7.2 0.8 convert_reduce_fusion.1
  8.1 0.9 select_reduce_fusion.1
  8.9 0.7 multiply_add_fusion
  9.6 1.3 select_reduce_fusion
  11.0 1.4 convolution_convert_fusion
  12.4 2.7 copy.96
  15.1 4.2 all-to-all-start.2
  19.3 0.7 convert_element_type.48
  20.1 0.1 copy.90
  20.2 1.1 convolution_convert_fusion.1
  21.4 1.0 copy.88
  22.4 25.4 %all-to-all-done.2 = bf16[4,3,16,6144]{3,2,1,0:T(8,128)(2,1)S(1)} async-done(((bf16[4,3,16,6144]{3,2,1,0:T(8,128)(2,1)}), bf16[4,3,16,6144]{3,2,1,0:T(8,128)(2,1)S(1)}, u32[]{:S(2)}, u32[]{:S(2)}) %all-to-all-start.2) | async-done | bytes 2359328 | tf_op jit(solution)/shard_map/all_to_all | solution.py:36
  47.8 3.5 all-to-all-start
  51.3 0.2 all-gather.2.cloned.1.call-start
  51.5 0.5 all-gather.2.cloned.1.call-update
  52.0 4.3 mul.109
  56.3 9.4 %mul.105 = bf16[48,128,16,128]{3,2,1,0:T(8,128)(2,1)} broadcast(bf16[48,16]{1,0:T(8,128)(2,1)S(1)} %copy.89), dimensions={0,2} | broadcast | bytes 25167360 | tf_op jit(solution)/shard_map/mul | solution.py:57
  65.7 43.0 %bitcast_multiply_fusion.1 = (bf16[6144,2048]{1,0:T(8,128)(2,1)}, bf16[6144,2048]{1,0:T(8,128)(2,1)}) fusion(bf16[768,8,16,128]{3,2,1,0:T(8,128)(2,1)S(1)} %bitcast.105, bf16[1,6144,2048]{2,1,0:T(8,128)(2,1)} %param.15, bf16[768,8,16,128]{3,2,1,0:T(8,128)(2,1)} %bitcast.106, bf16[1,6144,2048]{2,1,0:T(8,128)(2,1)} %param.14), kind=kLoop, calls=%fused_computation.7 | loop fusion | flops 25165824 | bytes 150994944 | tf_op jit(solution)/shard_map/mul | solution.py:61
  108.7 8.9 %mul.114 = bf16[16,128,48,128]{3,2,1,0:T(8,128)(2,1)} broadcast(bf16[16,48]{1,0:T(8,128)(2,1)S(1)} %get-tuple-element.43), dimensions={0,2} | broadcast | bytes 25167360 | tf_op jit(solution)/shard_map/mul | solution.py:64
  117.6 35.6 %mul.115 = bf16[1,2048,6144]{2,1,0:T(8,128)(2,1)} reshape(bf16[16,128,48,128]{3,2,1,0:T(8,128)(2,1)} %mul.114) | data formatting | bytes 50331648 | tf_op jit(solution)/shard_map/mul | solution.py:64
  153.2 0.4 fusion.50
  153.6 17.6 %fusion.14 = f32[12,4096]{1,0:T(8,128)S(1)} fusion(bf16[6144,2048]{1,0:T(8,128)(2,1)} %get-tuple-element.46, bf16[6144,2048]{1,0:T(8,128)(2,1)} %get-tuple-element.47, bf16[12,1,6144]{2,1,0:T(2,128)(2,1)S(1)} %get-tuple-element.39), kind=kOutput, calls=%fused_computation.18 | convolution fusion | flops 704643072 | bytes 50675712 | tf_op jit(solution)/shard_map/dot_general | solution.py:74
  171.2 18.1 %multiply_convert_fusion.1 = (bf16[12,2048]{1,0:T(8,128)(2,1)S(1)}, f32[12,2048]{1,0:T(8,128)S(1)}, bf16[12,2048]{1,0:T(8,128)(2,1)S(1)}, f32[12,2048]{1,0:T(8,128)S(1)}, bf16[12,2048]{1,0:T(8,128)(2,1)S(1)}) fusion(f32[12,4096]{1,0:T(8,128)S(1)} %fusion.14, bf16[1,2048,6144]{2,1,0:T(8,128)(2,1)} %param.16, bf16[1,2048,6144]{2,1,0:T(8,128)(2,1)} %mul.115, ...), kind=kOutput, calls=%fused_computation.48 | convolution fusion | flops 314941440 | bytes 51019776 | tf_op jit(solution)/shard_map/sd,hd->sh/dot_general | solution.py:86
  189.3 19.9 %fusion.13 = f32[12,6144]{1,0:T(8,128)S(1)} fusion(bf16[6144,2048]{1,0:T(8,128)(2,1)} %get-tuple-element.46, bf16[6144,2048]{1,0:T(8,128)(2,1)} %get-tuple-element.47, bf16[12,2048]{1,0:T(8,128)(2,1)S(1)} %get-tuple-element.38, bf16[12,2048]{1,0:T(8,128)(2,1)S(1)} %get-tuple-element.32), kind=kOutput, calls=%fused_computation.17 | convolution fusion | flops 704839680 | bytes 50724864 | tf_op jit(solution)/shard_map/sh,dh->sd/dot_general | solution.py:96
  209.2 0.1 stack.34
  209.4 0.2 copy.92
  209.6 16.8 %fusion.17 = f32[1,4,3,6144]{3,1,2,0:T(4,128)S(1)} fusion(bf16[1,2048,6144]{2,1,0:T(8,128)(2,1)} %param.16, bf16[1,2048,6144]{2,1,0:T(8,128)(2,1)} %mul.115, bf16[4,3,2048]{2,1,0:T(4,128)(2,1)S(1)} %reshape.80), kind=kOutput, calls=%fused_computation.23 | convolution fusion | flops 314572800 | bytes 50675712 | tf_op jit(solution)/shard_map/dot_general | solution.py:85
  226.4 0.1 pad_maximum_fusion.5
  226.5 1.3 copy.93
  227.8 4.4 all-to-all-start.1
  232.2 47.7 %fusion = f32[12,64,4096]{2,1,0:T(8,128)} fusion(bf16[12,64,6144]{2,1,0:T(8,128)(2,1)} %all-gather.2.cloned.1.call-done, bf16[6144,2048]{1,0:T(8,128)(2,1)} %get-tuple-element.46, bf16[6144,2048]{1,0:T(8,128)(2,1)} %get-tuple-element.47), kind=kOutput, calls=%fused_computation.1 | convolution fusion | flops 38755368960 | bytes 72351744 | tf_op jit(solution)/shard_map/srd,dh->srh/dot_general | solution.py:68
  279.9 32.4 %fusion.3 = f32[6144,12,64]{0,2,1:T(8,128)} fusion(bf16[256,8,48,128]{3,2,1,0:T(8,128)(2,1)} %bitcast.104, bf16[1,2048,6144]{2,1,0:T(8,128)(2,1)} %param.16, f32[12,64,4096]{2,1,0:T(8,128)} %fusion, f32[12,2048]{1,0:T(8,128)S(1)} %get-tuple-element.41, f32[12,2048]{1,0:T(8,128)S(1)} %get-tuple-element.33), kind=kOutput, calls=%fused_computation.5 | convolution fusion | flops 19383975936 | bytes 81985536 | tf_op jit(solution)/shard_map/srh,hd->rsd/dot_general | solution.py:98
  312.3 9.5 %slice_bitcast_fusion.3 = (f32[1,64,1,3,6144]{4,1,3,2,0:T(8,128)S(1)}, f32[1,64,1,3,6144]{4,1,3,2,0:T(8,128)S(1)}, f32[1,64,1,3,6144]{4,1,3,2,0:T(8,128)S(1)}, f32[1,64,1,3,6144]{4,1,3,2,0:T(8,128)}) fusion(f32[64,4,3,6144]{3,0,2,1:T(8,128)} %bitcast.107), kind=kLoop, calls=%fused_computation.32 | loop fusion | bytes 37748736 | tf_op jit(solution)/shard_map/stack | solution.py:105
  321.8 8.5 %pad_maximum_fusion.1 = f32[4,64,1,3,6144]{4,1,3,2,0:T(8,128)} fusion(f32[1,64,1,3,6144]{4,1,3,2,0:T(8,128)S(1)} %get-tuple-element.35, f32[1,64,1,3,6144]{4,1,3,2,0:T(8,128)S(1)} %get-tuple-element.36, f32[1,64,1,3,6144]{4,1,3,2,0:T(8,128)} %get-tuple-element.37, f32[1,64,1,3,6144]{4,1,3,2,0:T(8,128)S(1)} %get-tuple-element.34), kind=kLoop, calls=%fused_computation.16 | loop fusion | flops 14155776 | bytes 37748736 | tf_op jit(solution)/shard_map/stack | solution.py:105
  330.3 7.5 all-to-all-start.3
  337.8 0.3 all-reduce.4.cloned.1.call-start
  338.1 2.8 convolution_bitcast_fusion
  340.9 202.4 %all-to-all-done.3 = f32[4,64,1,3,6144]{4,1,3,2,0:T(8,128)} async-done(((f32[4,64,1,3,6144]{4,1,3,2,0:T(8,128)}), f32[4,64,1,3,6144]{4,1,3,2,0:T(8,128)}, u32[]{:S(2)}, u32[]{:S(2)}) %all-to-all-start.3) | async-done | bytes 18874400 | tf_op jit(solution)/shard_map/all_to_all | solution.py:104
  543.3 31.6 %fusion.11 = f32[4,64,6144]{2,0,1:T(4,128)} fusion(f32[64,12,6144]{2,0,1:T(8,128)} %bitcast.32, f32[4,12]{1,0:T(4,128)S(1)} %copy-done.3), kind=kOutput, calls=%fused_computation.14 | convolution fusion | flops 226492416 | bytes 25166016 | tf_op jit(solution)/shard_map/bs,rsd->brd/dot_general | solution.py:126
  575.0 0.6 dynamic-slice
  576.2 229.5 %all-reduce.4.cloned.1.call-done = (f32[2,4,6144]{2,1,0:T(4,128)}, f32[4,64,6144]{2,0,1:T(4,128)}) async-done(((f32[2,4,6144]{2,1,0:T(4,128)}, f32[4,64,6144]{2,0,1:T(4,128)}), (f32[2,4,6144]{2,1,0:T(4,128)}, f32[4,64,6144]{2,0,1:T(4,128)})) %all-reduce.4.cloned.1.call-update) | async-done | bytes 6488080 | tf_op jit(solution)/shard_map/psum | solution.py:139
  805.8 1.7 dynamic-slice_convert_fusion
  807.5 1.9 abs_reduce_fusion
  809.4 1.5 fusion.38
  810.9 1.5 slice_bitcast_fusion.4
  812.5 1.3 copy.99
  813.8 17.0 %psum.15 = bf16[4,6144]{1,0:T(4,128)(2,1)S(1)} all-reduce(bf16[4,6144]{1,0:T(4,128)(2,1)S(1)} %abs_reduce_fusion), channel_id=1, replica_groups=mesh['groups'=2,'tensor'=4,'expert'=4] {'tensor'}, use_global_device_ids=true, to_apply=%region_8.9 | all-reduce | flops 24576 | bytes 98304 | tf_op jit(solution)/shard_map/psum | solution.py:141
  830.8 0.7 convert_element_type.57
  (19 shorter events, 0.3 us)
Async XLA Ops:
  7.2 3.8 copy-start
  15.1 32.7 %all-to-all-start.2 = ((bf16[4,3,16,6144]{3,2,1,0:T(8,128)(2,1)}), bf16[4,3,16,6144]{3,2,1,0:T(8,128)(2,1)S(1)}, u32[]{:S(2)}, u32[]{:S(2)}) async-start(bf16[4,3,16,6144]{3,2,1,0:T(8,128)(2,1)} %bitcast.109), calls=%async_computation.2 | async-start | bytes 4718592 | tf_op jit(solution)/shard_map/all_to_all | solution.py:36
  47.8 3.7 copy-start.2
  47.8 105.4 %all-to-all-start = ((bf16[4,3,2,6144]{3,2,1,0:T(2,128)(2,1)}), bf16[4,3,2,6144]{3,2,1,0:T(2,128)(2,1)S(1)}, u32[]{:S(2)}, u32[]{:S(2)}) async-start(bf16[4,3,2,6144]{3,2,1,0:T(2,128)(2,1)} %bitcast.3), calls=%async_computation | async-start | bytes 589824 | tf_op jit(solution)/shard_map/all_to_all | solution.py:43
  51.3 180.9 %all-gather.2.cloned.1.call-start = ((), (), s32[]{:S(2)}) async-start(), calls=%async_computation.4 | async-start | bytes 11796480 | tf_op jit(solution)/shard_map/all_gather | solution.py:70
  227.8 102.5 %all-to-all-start.1 = ((f32[2,4,3,6144]{3,0,2,1:T(2,128)}), f32[2,4,3,6144]{3,0,2,1:T(2,128)}, u32[]{:S(2)}, u32[]{:S(2)}) async-start(f32[2,4,3,6144]{3,0,2,1:T(2,128)} %copy.93), calls=%async_computation.1 | async-start | bytes 1179648 | tf_op jit(solution)/shard_map/all_to_all | solution.py:118
  330.3 7.8 copy-start.3
  330.3 213.0 %all-to-all-start.3 = ((f32[4,64,1,3,6144]{4,1,3,2,0:T(8,128)}), f32[4,64,1,3,6144]{4,1,3,2,0:T(8,128)}, u32[]{:S(2)}, u32[]{:S(2)}) async-start(f32[4,64,1,3,6144]{4,1,3,2,0:T(8,128)} %pad_maximum_fusion.1), calls=%async_computation.3 | async-start | bytes 37748736 | tf_op jit(solution)/shard_map/all_to_all | solution.py:104
  337.8 237.2 %copy-start.4 = (u32[32]{0:T(128)S(1)}, u32[32]{0:T(128)}, u32[]{:S(2)}) copy-start(u32[32]{0:T(128)} %constant.24) | copy-start | bytes 388
  337.8 493.7 %copy-start.1 = (bf16[4,16,6144]{2,1,0:T(8,128)(2,1)S(1)}, bf16[4,16,6144]{2,1,0:T(8,128)(2,1)}, u32[]{:S(2)}) copy-start(bf16[4,16,6144]{2,1,0:T(8,128)(2,1)} %param.10) | copy-start | bytes 2359300
  337.8 468.0 %all-reduce.4.cloned.1.call-start = ((), (), s32[]{:S(2)}) async-start(), calls=%async_computation.5 | async-start | bytes 12976128 | tf_op jit(solution)/shard_map/psum | solution.py:139
Sparse Core Ops, SparseCore 0:
  53.7 169.3 all-gather.1
  575.1 230.6 all-reduce.3
